TPU v7x, 32 devices: a whole 2x2x4 slice. The times are simulated.
32 devices in a mesh: node: 8 (over z, x), local: 4 (over y, core).
Axes of the slice: x: 2, y: 2, z: 4, core: 2. Of those that a mesh axis runs over, the one named last changes fastest.
Arguments:
- tokens: bfloat16 [64, 4096], P('node', 'local'), may hold values from -6 to 6
- cotangent: bfloat16 [64, 4096], P('node', 'local'), may hold values from -6 to 6
- expert_ids: int32 [64, 8], P('node'), may hold values from 0 to 7, as said below
- combine_weights: float32 [64, 8], P('node'), may hold values from 0.1 to 1
- w_gate: bfloat16 [8, 4096, 2048], P('node', None, 'local'), may hold values from -0.09375 to 0.09375
- w_up: bfloat16 [8, 4096, 2048], P('node', None, 'local'), may hold values from -0.09375 to 0.09375
- w_down: bfloat16 [8, 2048, 4096], P('node', 'local'), may hold values from -0.125 to 0.125
Outputs:
- layer_out: bfloat16 [64, 4096], P('node', 'local')
- token_grad: bfloat16 [64, 4096], P('node', 'local')
- weight_grad: float32 [64, 8], P('node')
Inputs may be any that keep to these rules, and one draw needn't show every extreme that they name: `expert_ids`: each row names 8 different experts, all of them in at most 4 groups of 8 consecutive experts.
All inputs are finite; a program needn't handle non-finite values.
Results may differ from a plain program's by a relative error of at most 0.012.
Values may be sent and summed in bfloat16 or wider, within the bound.
A program may use at most 64 MiB of HBM per device.

v0:
```python
import jax
import jax.numpy as jnp
from jax import lax
from jax.sharding import PartitionSpec as P


def swiglu_parts(gate_pre, up_pre, grad_hidden):
    sigmoid = jax.nn.sigmoid(gate_pre)
    activated = gate_pre * sigmoid
    hidden = (activated * up_pre).astype(jnp.bfloat16)
    slope = sigmoid * (1.0 + gate_pre * (1.0 - sigmoid))
    grad_gate = (grad_hidden * up_pre * slope).astype(jnp.bfloat16)
    grad_up = (grad_hidden * activated).astype(jnp.bfloat16)
    return (hidden, grad_gate, grad_up)


def body(tokens, cotangent, expert_ids, combine_weights, w_gate, w_up, w_down):
    experts = lax.axis_size("node")
    node_tokens, width_local = tokens.shape
    top_count = expert_ids.shape[1]
    capacity = min(node_tokens, (3 * node_tokens * top_count + 2 * experts - 1) // (2 * experts))
    row_total = experts * capacity
    matches = (expert_ids[:, :, None] == lax.iota(jnp.int32, experts)[None, None, :]).astype(
        jnp.int32
    )
    routed = jnp.sum(matches, axis=1)
    position = jnp.cumsum(routed, axis=0) - routed
    kept = routed * (position < capacity).astype(jnp.int32)
    slot_ids = lax.iota(jnp.int32, capacity)
    select_mask = (kept.T[:, None, :] == 1) & (position.T[:, None, :] == slot_ids[None, :, None])
    select_float = select_mask.astype(jnp.float32)
    select_half = select_mask.astype(jnp.bfloat16)
    send_tok = jnp.einsum(
        "epi,id->epd", select_half, tokens, preferred_element_type=jnp.float32
    ).astype(jnp.bfloat16)
    send_cot = jnp.einsum(
        "epi,id->epd", select_half, cotangent, preferred_element_type=jnp.float32
    ).astype(jnp.bfloat16)
    recv_tok, recv_cot = (
        lax.all_to_all(send_tok, "node", split_axis=0, concat_axis=0, tiled=True),
        lax.all_to_all(send_cot, "node", split_axis=0, concat_axis=0, tiled=True),
    )
    weight_gate = w_gate[0]
    weight_up = w_up[0]
    weight_down = w_down[0]
    full_tok, full_cot = (
        lax.all_gather(recv_tok, "local", axis=2, tiled=True),
        lax.all_gather(recv_cot, "local", axis=2, tiled=True),
    )
    flat_tok = full_tok.reshape(row_total, -1)
    flat_cot = full_cot.reshape(row_total, -1)
    gate_pre = jnp.dot(flat_tok, weight_gate, preferred_element_type=jnp.float32)
    up_pre = jnp.dot(flat_tok, weight_up, preferred_element_type=jnp.float32)
    grad_hidden = jnp.einsum("rd,fd->rf", flat_cot, weight_down, preferred_element_type=jnp.float32)
    hidden, grad_gate, grad_up = swiglu_parts(gate_pre, up_pre, grad_hidden)
    output_part = jnp.einsum("fc,rf->cr", weight_down, hidden, preferred_element_type=jnp.float32)
    input_part = jnp.einsum("cf,rf->cr", weight_gate, grad_gate, preferred_element_type=jnp.float32)
    input_part = input_part + jnp.einsum(
        "cf,rf->cr", weight_up, grad_up, preferred_element_type=jnp.float32
    )
    summed = lax.psum_scatter(
        jnp.concatenate([output_part, input_part], axis=1).astype(jnp.bfloat16),
        "local",
        scatter_dimension=0,
        tiled=True,
    )
    outgoing = summed.reshape(width_local, 2, experts, capacity)
    returned = lax.all_to_all(outgoing, "node", split_axis=2, concat_axis=2, tiled=True)
    returned_float = returned.astype(jnp.float32)
    gate_table = jnp.sum(combine_weights[:, :, None] * matches.astype(jnp.float32), axis=1)
    weighted = select_float * gate_table.T[:, None, :]
    layer_out = jnp.einsum("epi,cep->ic", weighted, returned_float[:, 0]).astype(jnp.bfloat16)
    token_grad = jnp.einsum("epi,cep->ic", weighted, returned_float[:, 1]).astype(jnp.bfloat16)
    slot_inner = jnp.einsum("cep,epc->ep", returned_float[:, 0], send_cot.astype(jnp.float32))
    inner = jnp.einsum("epi,ep->ie", select_float, slot_inner)
    partial_grad = jnp.sum(inner[:, None, :] * matches.astype(jnp.float32), axis=2)
    weight_grad = lax.psum(partial_grad, "local")
    return (layer_out, token_grad, weight_grad)


def solution(mesh):
    in_specs = (
        P("node", "local"),
        P("node", "local"),
        P("node", None),
        P("node", None),
        P("node", None, "local"),
        P("node", None, "local"),
        P("node", "local", None),
    )
    out_specs = (P("node", "local"), P("node", "local"), P("node", None))
    return jax.shard_map(body, mesh=mesh, in_specs=in_specs, out_specs=out_specs, check_vma=False)
```

profile of v0, /device:TPU:0, one launch (start us, length us, event | category | flops | bytes accessed | tf_op | source)
XLA Modules:
  0.0 111.8 jit_solution(6429937621670824099)
XLA Ops:
  7.2 0.8 convert_reduce_fusion
  8.2 0.9 convolution_convert_fusion.2
  9.1 7.3 %all-to-all-start = ((bf16[8,8,1024]{2,1,0:T(8,128)(2,1)}), bf16[8,8,1024]{2,1,0:T(8,128)(2,1)S(1)}, u32[]{:S(2)}, u32[]{:S(2)}) async-start(bf16[8,8,1024]{2,1,0:T(8,128)(2,1)} %convolution_convert_fusion.2), calls=%async_computation | async-start | bytes 262144 | tf_op jit(solution)/shard_map/all_to_all | solution.py:40
  16.3 1.7 %convolution_convert_fusion.1 = bf16[8,8,1024]{2,1,0:T(8,128)(2,1)} fusion(bf16[8,1024]{1,0:T(8,128)(2,1)} %param.8, s32[8,8]{1,0:T(8,128)S(1)} %copy.18, pred[8,8]{1,0:T(8,128)(4,1)S(1)} %copy.17), kind=kOutput, calls=%fused_computation.15 | convolution fusion | flops 1115136 | bytes 147776 | tf_op jit(solution)/shard_map/epi,id->epd/dot_general | solution.py:36
  18.0 5.7 %all-to-all-done = bf16[8,8,1024]{2,1,0:T(8,128)(2,1)S(1)} async-done(((bf16[8,8,1024]{2,1,0:T(8,128)(2,1)}), bf16[8,8,1024]{2,1,0:T(8,128)(2,1)S(1)}, u32[]{:S(2)}, u32[]{:S(2)}) %all-to-all-start) | async-done | bytes 131104 | tf_op jit(solution)/shard_map/all_to_all | solution.py:40
  23.7 3.4 %all-to-all-start.1 = ((bf16[8,8,1024]{2,1,0:T(8,128)(2,1)}), bf16[8,8,1024]{2,1,0:T(8,128)(2,1)S(1)}, u32[]{:S(2)}, u32[]{:S(2)}) async-start(bf16[8,8,1024]{2,1,0:T(8,128)(2,1)} %convolution_convert_fusion.1), calls=%async_computation.1 | async-start | bytes 262144 | tf_op jit(solution)/shard_map/all_to_all | solution.py:41
  27.1 7.3 %all_gather.6 = bf16[8,8,4096]{2,1,0:T(8,128)(2,1)S(1)} all-gather(bf16[8,8,1024]{2,1,0:T(8,128)(2,1)S(1)} %all-to-all-done), channel_id=1, replica_groups=mesh['node'=8,'local'=4] {'local'}, dimensions={2}, use_global_device_ids=true | all-gather | bytes 655360 | tf_op jit(solution)/shard_map/all_gather | solution.py:47
  34.5 3.0 %fusion.11 = f32[64,512]{1,0:T(8,128)S(1)} fusion(bf16[1,4096,512]{2,1,0:T(8,128)(2,1)} %param.11, bf16[8,8,4096]{2,1,0:T(8,128)(2,1)S(1)} %all_gather.6), kind=kOutput, calls=%fused_computation.13 | convolution fusion | flops 268435456 | bytes 4849664 | tf_op jit(solution)/shard_map/dot_general | solution.py:52
  37.5 0.8 fusion.7
  38.4 7.4 %all_gather.7 = bf16[8,8,4096]{2,1,0:T(8,128)(2,1)S(1)} all-gather(bf16[8,8,1024]{2,1,0:T(8,128)(2,1)S(1)} %all-to-all-done.1), channel_id=1, replica_groups=mesh['node'=8,'local'=4] {'local'}, dimensions={2}, use_global_device_ids=true | all-gather | bytes 655360 | tf_op jit(solution)/shard_map/all_gather | solution.py:48
  45.8 3.7 %fusion.3 = f32[64,512]{1,0:T(8,128)S(1)} fusion(bf16[1,512,4096]{2,1,0:T(8,128)(2,1)} %param.13, bf16[8,8,4096]{2,1,0:T(8,128)(2,1)S(1)} %all_gather.7), kind=kOutput, calls=%fused_computation.5 | convolution fusion | flops 268435456 | bytes 4849664 | tf_op jit(solution)/shard_map/rd,fd->rf/dot_general | solution.py:54
  49.5 0.8 fusion.2
  50.4 1.4 %fusion.9 = f32[64,4096]{1,0:T(8,128)S(1)} fusion(bf16[1,4096,512]{2,1,0:T(8,128)(2,1)S(1)} %copy-done.2, f32[64,512]{1,0:T(8,128)S(1)} %fusion.11, f32[64,512]{1,0:T(8,128)S(1)} %fusion.3, f32[64,512]{1,0:T(8,128)S(1)} %fusion.7), kind=kOutput, calls=%fused_computation.11 | convolution fusion | flops 268763136 | bytes 5636096 | tf_op jit(solution)/shard_map/cf,rf->cr/dot_general | solution.py:57
  51.8 1.4 %fusion.1 = bf16[4096,64]{0,1:T(8,128)(2,1)S(1)} fusion(f32[64,4096]{1,0:T(8,128)S(1)} %fusion.9, bf16[1,4096,512]{2,1,0:T(8,128)(2,1)S(1)} %copy-done.4, f32[64,512]{1,0:T(8,128)S(1)} %fusion.3, f32[64,512]{1,0:T(8,128)S(1)} %fusion.11), kind=kOutput, calls=%fused_computation.3 | convolution fusion | flops 269156352 | bytes 6029312 | tf_op jit(solution)/shard_map/cf,rf->cr/dot_general | solution.py:58
  53.2 1.1 pad_maximum_fusion
  54.3 25.7 %reduce-scatter.2.cloned.1.call-done = bf16[1024,128]{0,1:T(8,128)(2,1)} async-done(((bf16[4096,128]{0,1:T(8,128)(2,1)}), bf16[1024,128]{0,1:T(8,128)(2,1)}) %reduce-scatter.2.cloned.1.call-update) | async-done | bytes 262160 | tf_op jit(solution)/shard_map/reduce_scatter | solution.py:61
  80.0 1.0 copy.22
  80.9 14.2 %all_to_all.15 = bf16[1024,2,8,8]{0,3,1,2:T(8,128)(2,1)S(1)} all-to-all(bf16[1024,2,8,8]{0,3,1,2:T(8,128)(2,1)S(1)} %copy.22), channel_id=1, replica_groups=mesh['node'=8,'local'=4] {'node'}, dimensions={2} | all-to-all | bytes 524288 | tf_op jit(solution)/shard_map/all_to_all | solution.py:68
  95.2 1.0 fusion.18
  96.2 0.2 fusion.31
  96.5 0.2 fusion.28
  96.7 6.5 %psum.7 = f32[8,8]{1,0:T(8,128)} all-reduce(f32[8,8]{1,0:T(8,128)S(1)} %get-tuple-element.3), channel_id=1, replica_groups=mesh['node'=8,'local'=4] {'local'}, use_global_device_ids=true, to_apply=%region_5.6 | all-reduce | flops 64 | bytes 512 | tf_op jit(solution)/shard_map/psum | solution.py:77
  103.2 0.9 fusion.14
  104.1 0.9 fusion.13
  (23 shorter events, 0.4 us)
Async XLA Ops:
  7.2 1.0 copy-start
  9.1 14.6 %all-to-all-start = ((bf16[8,8,1024]{2,1,0:T(8,128)(2,1)}), bf16[8,8,1024]{2,1,0:T(8,128)(2,1)S(1)}, u32[]{:S(2)}, u32[]{:S(2)}) async-start(bf16[8,8,1024]{2,1,0:T(8,128)(2,1)} %convolution_convert_fusion.2), calls=%async_computation | async-start | bytes 262144 | tf_op jit(solution)/shard_map/all_to_all | solution.py:40
  23.7 14.6 %all-to-all-start.1 = ((bf16[8,8,1024]{2,1,0:T(8,128)(2,1)}), bf16[8,8,1024]{2,1,0:T(8,128)(2,1)S(1)}, u32[]{:S(2)}, u32[]{:S(2)}) async-start(bf16[8,8,1024]{2,1,0:T(8,128)(2,1)} %convolution_convert_fusion.1), calls=%async_computation.1 | async-start | bytes 262144 | tf_op jit(solution)/shard_map/all_to_all | solution.py:41
  27.1 52.9 %reduce-scatter.2.cloned.1.call-start = ((), (), s32[]{:S(2)}) async-start(), calls=%async_computation.4 | async-start | bytes 1310720 | tf_op jit(solution)/shard_map/reduce_scatter | solution.py:61
  27.1 10.4 %copy-start.3 = (bf16[1,4096,512]{2,1,0:T(8,128)(2,1)S(1)}, bf16[1,4096,512]{2,1,0:T(8,128)(2,1)}, u32[]{:S(2)}) copy-start(bf16[1,4096,512]{2,1,0:T(8,128)(2,1)} %param.12) | copy-start | bytes 12582916
  38.3 11.2 %copy-start.1 = (bf16[1,512,4096]{2,1,0:T(8,128)(2,1)S(1)}, bf16[1,512,4096]{2,1,0:T(8,128)(2,1)}, u32[]{:S(2)}) copy-start(bf16[1,512,4096]{2,1,0:T(8,128)(2,1)} %param.13) | copy-start | bytes 12582916
  45.8 4.6 %copy-start.2 = (bf16[1,4096,512]{2,1,0:T(8,128)(2,1)S(1)}, bf16[1,4096,512]{2,1,0:T(8,128)(2,1)}, u32[]{:S(2)}) copy-start(bf16[1,4096,512]{2,1,0:T(8,128)(2,1)} %param.11) | copy-start | bytes 12582916
  49.5 2.2 %copy-start.4 = (bf16[1,4096,512]{2,1,0:T(8,128)(2,1)S(1)}, bf16[1,4096,512]{2,1,0:T(8,128)(2,1)}, u32[]{:S(2)}) copy-start(bf16[1,4096,512]{2,1,0:T(8,128)(2,1)} %param.12) | copy-start | bytes 12582916
  51.8 44.7 %copy-start.5 = (s32[8,8]{1,0:T(8,128)S(1)}, s32[8,8]{1,0:T(8,128)}, u32[]{:S(2)}) copy-start(s32[8,8]{1,0:T(8,128)} %param.9) | copy-start | bytes 772
  51.8 44.7 %copy-start.6 = (f32[8,8]{1,0:T(8,128)S(1)}, f32[8,8]{1,0:T(8,128)}, u32[]{:S(2)}) copy-start(f32[8,8]{1,0:T(8,128)} %param.10) | copy-start | bytes 772
Sparse Core Ops, SparseCore 0:
  54.4 25.5 reduce-scatter.1
where the time goes:
time: 112 us
  blocking collectives  35.5 us (32%)
  waiting for transfers between devices  31.4 us (28%)
  matrix products  15.8 us (14%)
  between operations  14.2 us (13%)
  starting transfers between devices  10.7 us (10%)
  other arithmetic  3.07 us (3%)
  local copies, waits for them, and re-layouts  1.32 us (1%)
    reduce_scatter x1, waiting for transfers between devices, body(): lax.psum_scatter(jnp.concatenate([output_part, input_part], axis=1).astyp...  25.7 us
    all_to_all x1, blocking collectives, body(): lax.all_to_all(outgoing, 'node', split_axis=2, concat_axis=2, tiled=True)  14.2 us
    all_gather x1, blocking collectives, body(): lax.all_gather(recv_cot, 'local', axis=2, tiled=True)  7.42 us
    all_gather x1, blocking collectives, body(): lax.all_gather(recv_tok, 'local', axis=2, tiled=True)  7.33 us
    all_to_all x1, starting transfers between devices, body(): lax.all_to_all(send_tok, 'node', split_axis=0, concat_axis=0, tiled=True)  7.25 us
    psum x1, blocking collectives, body(): weight_grad = lax.psum(partial_grad, 'local')  6.49 us
    all_to_all x1, waiting for transfers between devices, body(): lax.all_to_all(send_tok, 'node', split_axis=0, concat_axis=0, tiled=True)  5.69 us
    dot_general x1, matrix products, body(): jnp.einsum('rd,fd->rf', flat_cot, weight_down, preferred_element_type=jnp...  3.75 us
  transfers between devices with their start and end apart: 3, of which 2 were waited for; matrix products, arithmetic and copies ran while one was open for 5% of the time, Pallas kernels for 0%

commit v1 on v0

--- a/solution.py
+++ b/solution.py
@@ -1,6 +1,10 @@
+import functools
+
 import jax
 import jax.numpy as jnp
 from jax import lax
+from jax.experimental import pallas as pl
+from jax.experimental.pallas import tpu as pltpu
 from jax.sharding import PartitionSpec as P
 
 
@@ -14,7 +18,7 @@
     return (hidden, grad_gate, grad_up)
 
 
-def body(tokens, cotangent, expert_ids, combine_weights, w_gate, w_up, w_down):
+def general_body(tokens, cotangent, expert_ids, combine_weights, w_gate, w_up, w_down):
     experts = lax.axis_size("node")
     node_tokens, width_local = tokens.shape
     top_count = expert_ids.shape[1]
@@ -78,6 +82,315 @@
     return (layer_out, token_grad, weight_grad)
 
 
+MESH = pl.DeviceIdType.MESH
+NT = (((1,), (1,)), ((), ()))
+NN = (((1,), (0,)), ((), ()))
+
+
+def mm(a, b, dims):
+    return lax.dot_general(a, b, dims, preferred_element_type=jnp.float32)
+
+
+def fused_kernel(
+    nodes,
+    tok_ref,
+    cot_ref,
+    ids_ref,
+    cw_ref,
+    wg_hbm,
+    wu_hbm,
+    wd_hbm,
+    lo_ref,
+    tg_ref,
+    wgrad_ref,
+    wg_v,
+    wu_v,
+    wd_v,
+    xb,
+    gt,
+    rl,
+    rn_s,
+    rn,
+    mate_s,
+    mate_r,
+    y_s,
+    y_r,
+    n_s,
+    n_r,
+    part,
+    w_sem,
+    xs_sem,
+    xr_sem,
+    gs_sem,
+    gr_sem,
+    ls_sem,
+    lr_sem,
+    ns_sem,
+    nr_sem,
+    ms_sem,
+    mr_sem,
+    ys_sem,
+    yr_sem,
+    os_sem,
+    or_sem,
+):
+    me = lax.axis_index("node")
+    l = lax.axis_index("local")
+    core = lax.rem(l, 2)
+    mate = l + 1 - 2 * core
+    ymate = lax.rem(l + 2, 4)
+    diag = lax.rem(mate + 2, 4)
+    order = (l, mate, ymate, diag)
+    toks, width = tok_ref.shape
+    rows = nodes * toks
+
+    def peer(d):
+        return lax.rem(me + d, nodes)
+
+    def source(d):
+        return lax.rem(me - d + nodes, nodes)
+
+    w_copies = []
+    for j, c in enumerate(order):
+        cols = pl.ds(pl.multiple_of(c * width, width), width)
+        group = (
+            pltpu.make_async_copy(wg_hbm.at[0, cols, :], wg_v.at[c], w_sem.at[0, j]),
+            pltpu.make_async_copy(wu_hbm.at[0, cols, :], wu_v.at[c], w_sem.at[1, j]),
+            pltpu.make_async_copy(wd_hbm.at[0, :, cols], wd_v.at[c], w_sem.at[2, j]),
+        )
+        for copy in group:
+            copy.start()
+        w_copies.append(group)
+
+    barrier = pltpu.get_barrier_semaphore()
+    for d in range(1, nodes):
+        pl.semaphore_signal(barrier, inc=1, device_id=(peer(d), l), device_id_type=MESH)
+    for c in (mate, ymate, diag):
+        pl.semaphore_signal(barrier, inc=1, device_id=(me, c), device_id_type=MESH)
+
+    xb[l, me] = jnp.concatenate(
+        [tok_ref[...].astype(jnp.float32), cot_ref[...].astype(jnp.float32)], axis=0
+    ).astype(jnp.bfloat16)
+    ids = ids_ref[...]
+    lanes = lax.broadcasted_iota(jnp.int32, (toks, 128), 1)
+    table = jnp.zeros((toks, 128), jnp.float32)
+    for k in range(ids.shape[1]):
+        table = table + jnp.where(lanes == ids[:, k : k + 1], cw_ref[:, k : k + 1], 0.0)
+    gt[me] = table
+
+    pl.semaphore_wait(barrier, nodes + 2)
+
+    sends = []
+
+    def send(src, dst, ssem, rsem, device):
+        copy = pltpu.make_async_remote_copy(
+            src_ref=src,
+            dst_ref=dst,
+            send_sem=ssem,
+            recv_sem=rsem,
+            device_id=device,
+            device_id_type=MESH,
+        )
+        copy.start()
+        sends.append(copy)
+        return copy
+
+    x_node = [None]
+    g_node = [None]
+    for d in range(1, nodes):
+        x_node.append(
+            send(xb.at[l, me], xb.at[l, me], xs_sem.at[0, d], xr_sem.at[0, d], (peer(d), l))
+        )
+    x_mate, x_y, x_diag = [], [], []
+
+    def onward(d):
+        block = xb.at[l, source(d)]
+        x_y.append(send(block, block, xs_sem.at[1, d], xr_sem.at[1, d], (me, ymate)))
+        x_mate.append(send(block, block, xs_sem.at[2, d], xr_sem.at[2, d], (me, mate)))
+
+    def relay(d):
+        x_y[d].wait_recv()
+        block = xb.at[ymate, source(d)]
+        x_diag.append(send(block, block, xs_sem.at[3, d], xr_sem.at[3, d], (me, mate)))
+
+    onward(0)
+    for d in range(1, nodes):
+        g_node.append(send(gt.at[me], gt.at[me], gs_sem.at[d], gr_sem.at[d], (peer(d), l)))
+    for d in range(1, nodes):
+        x_node[d].wait_recv()
+        onward(d)
+        relay(d - 1)
+    relay(nodes - 1)
+
+    gate_pre = up_pre = grad_hidden = None
+    for j, c in enumerate(order):
+        for copy in w_copies[j]:
+            copy.wait()
+        if j == 1:
+            for copy in x_mate:
+                copy.wait_recv()
+        if j == 3:
+            for copy in x_diag:
+                copy.wait_recv()
+        both = xb[c].astype(jnp.float32).reshape(nodes, 2, toks, width)
+        tok = both[:, 0].reshape(rows, width).astype(jnp.bfloat16)
+        cot = both[:, 1].reshape(rows, width).astype(jnp.bfloat16)
+        a = mm(tok, wg_v[c], NN)
+        b = mm(tok, wu_v[c], NN)
+        g = mm(cot, wd_v[c], NT)
+        if j == 0:
+            gate_pre, up_pre, grad_hidden = a, b, g
+        else:
+            gate_pre, up_pre, grad_hidden = gate_pre + a, up_pre + b, grad_hidden + g
+
+    for copy in g_node[1:]:
+        copy.wait_recv()
+    lanes3 = lax.broadcasted_iota(jnp.int32, (nodes, toks, 128), 2)
+    scale = jnp.sum(jnp.where(lanes3 == me, gt[...], 0.0), axis=2, keepdims=True).reshape(rows, 1)
+    sigmoid = jax.nn.sigmoid(gate_pre)
+    activated = gate_pre * sigmoid
+    hidden = activated * up_pre
+    slope = sigmoid * (1.0 + gate_pre * (1.0 - sigmoid))
+    inner = jnp.sum(hidden * grad_hidden, axis=1, keepdims=True).reshape(nodes, toks, 1)
+    nodes3 = lax.broadcasted_iota(jnp.int32, (nodes, toks, 128), 0)
+    rl[l] = jnp.sum(jnp.where(lanes3 == nodes3, inner, 0.0), axis=0)
+    r_local = []
+    for j, c in enumerate((mate, ymate, diag)):
+        r_local.append(send(rl.at[l], rl.at[l], ls_sem.at[j], lr_sem.at[j], (me, c)))
+    scaled = grad_hidden * scale
+    hid = (hidden * scale).astype(jnp.bfloat16)
+    ggate = (scaled * up_pre * slope).astype(jnp.bfloat16)
+    gup = (scaled * activated).astype(jnp.bfloat16)
+
+    def partial(c):
+        out = mm(hid, wd_v[c], NN).reshape(nodes, toks, width)
+        into = (mm(ggate, wg_v[c], NT) + mm(gup, wu_v[c], NT)).reshape(nodes, toks, width)
+        return jnp.concatenate([out, into], axis=1)
+
+    def to_mate(i, c):
+        mate_s[i] = partial(c).astype(jnp.bfloat16)
+        return send(mate_s.at[i], mate_r.at[i], ms_sem.at[i], mr_sem.at[i], (me, mate))
+
+    first = to_mate(0, diag)
+    part[...] = partial(ymate)
+    first.wait_recv()
+    y_s[...] = (part[...] + mate_r[0].astype(jnp.float32)).astype(jnp.bfloat16)
+    turns = list(range(1, nodes)) + [0]
+    y_copies = {}
+    for d in turns:
+        n = peer(d)
+        y_copies[d] = send(y_s.at[n], y_r.at[n], ys_sem.at[d], yr_sem.at[d], (me, ymate))
+    second = to_mate(1, mate)
+    part[...] = partial(l)
+
+    for copy in r_local:
+        copy.wait_recv()
+    r_sum = rl[0] + rl[1] + rl[2] + rl[3]
+    r_node = []
+    for d in turns:
+        n = peer(d)
+        column = jnp.sum(jnp.where(lanes == n, r_sum, 0.0), axis=1, keepdims=True)
+        rn_s[d] = jnp.where(lanes == me, column, 0.0)
+        if d:
+            r_node.append(send(rn_s.at[d], rn.at[me], ns_sem.at[d], nr_sem.at[d], (n, l)))
+
+    second.wait_recv()
+    o_node = []
+    total = None
+    for d in turns:
+        n = peer(d)
+        y_copies[d].wait_recv()
+        value = part[n] + mate_r[1, n].astype(jnp.float32) + y_r[n].astype(jnp.float32)
+        if d:
+            n_s[d] = value.astype(jnp.bfloat16)
+            o_node.append(send(n_s.at[d], n_r.at[me], os_sem.at[d], or_sem.at[d], (n, l)))
+        else:
+            total = value
+    r_total = rn_s[0]
+    for i, d in enumerate(range(1, nodes)):
+        r_node[i].wait_recv()
+        r_total = r_total + rn[source(d)]
+    answer = jnp.zeros(ids.shape, jnp.float32)
+    slots = lax.broadcasted_iota(jnp.int32, ids.shape, 1)
+    for k in range(ids.shape[1]):
+        value = jnp.sum(jnp.where(lanes == ids[:, k : k + 1], r_total, 0.0), axis=1, keepdims=True)
+        answer = answer + jnp.where(slots == k, value, 0.0)
+    wgrad_ref[...] = answer
+    for i, d in enumerate(range(1, nodes)):
+        o_node[i].wait_recv()
+        total = total + n_r[source(d)].astype(jnp.float32)
+    lo_ref[...] = total[:toks].astype(jnp.bfloat16)
+    tg_ref[...] = total[toks:].astype(jnp.bfloat16)
+    for copy in sends:
+        copy.wait_send()
+
+
+def fused_body(tokens, cotangent, expert_ids, combine_weights, w_gate, w_up, w_down):
+    nodes = lax.axis_size("node")
+    toks, width = tokens.shape
+    units = w_gate.shape[2]
+    half, single = jnp.bfloat16, jnp.float32
+    block = (nodes, 2 * toks, width)
+    dma = pltpu.SemaphoreType.DMA
+    vmem = pl.BlockSpec(memory_space=pltpu.VMEM)
+    hbm = pl.BlockSpec(memory_space=pl.ANY)
+    return pl.pallas_call(
+        functools.partial(fused_kernel, nodes),
+        out_shape=(
+            jax.ShapeDtypeStruct((toks, width), half),
+            jax.ShapeDtypeStruct((toks, width), half),
+            jax.ShapeDtypeStruct(expert_ids.shape, single),
+        ),
+        in_specs=[vmem] * 4 + [hbm] * 3,
+        out_specs=(vmem, vmem, vmem),
+        scratch_shapes=[
+            pltpu.VMEM((4, width, units), half),
+            pltpu.VMEM((4, width, units), half),
+            pltpu.VMEM((4, units, width), half),
+            pltpu.VMEM((4,) + block, half),
+            pltpu.VMEM((nodes, toks, 128), single),
+            pltpu.VMEM((4, toks, 128), single),
+            pltpu.VMEM((nodes, toks, 128), single),
+            pltpu.VMEM((nodes, toks, 128), single),
+            pltpu.VMEM((2,) + block, half),
+            pltpu.VMEM((2,) + block, half),
+            pltpu.VMEM(block, half),
+            pltpu.VMEM(block, half),
+            pltpu.VMEM(block, half),
+            pltpu.VMEM(block, half),
+            pltpu.VMEM(block, single),
+            dma((3, 4)),
+            dma((4, nodes)),
+            dma((4, nodes)),
+            dma((nodes,)),
+            dma((nodes,)),
+            dma((3,)),
+            dma((3,)),
+            dma((nodes,)),
+            dma((nodes,)),
+            dma((2,)),
+            dma((2,)),
+            dma((nodes,)),
+            dma((nodes,)),
+            dma((nodes,)),
+            dma((nodes,)),
+        ],
+        compiler_params=pltpu.CompilerParams(
+            collective_id=0, has_side_effects=True, vmem_limit_bytes=44 * 1024 * 1024
+        ),
+    )(tokens, cotangent, expert_ids, combine_weights, w_gate, w_up, w_down)
+
+
+def body(tokens, cotangent, expert_ids, combine_weights, w_gate, w_up, w_down):
+    experts = lax.axis_size("node")
+    node_tokens = tokens.shape[0]
+    top_count = expert_ids.shape[1]
+    capacity = min(node_tokens, (3 * node_tokens * top_count + 2 * experts - 1) // (2 * experts))
+    whole = capacity == node_tokens and node_tokens == 8 and experts <= 128
+    chosen = fused_body if whole and lax.axis_size("local") == 4 else general_body
+    return chosen(tokens, cotangent, expert_ids, combine_weights, w_gate, w_up, w_down)
+
+
 def solution(mesh):
     in_specs = (
         P("node", "local"),

time: 112 us -> 50 us (0.45)
  Pallas kernels: 0 us -> 40 us
  blocking collectives: 35.5 us -> 0 us
  waiting for transfers between devices: 31.4 us -> 0 us
  matrix products: 15.8 us -> 0 us
  between operations: 14.2 us -> 0.66 us
  starting transfers between devices: 10.7 us -> 0 us
  local copies, waits for them, and re-layouts: 1.32 us -> 8.98 us
  other arithmetic: 3.07 us -> 0 us
    pallas_call x0 -> x1, Pallas kernels: none -> 40 us  [fused_body(): pl.pallas_call(functools.partial(fused_kernel, nodes), out_shape=(jax.Sha...]
    reduce_scatter x1 -> x0, waiting for transfers between devices: 25.7 us -> none  [body(): lax.psum_scatter(jnp.concatenate([output_part, input_part], axis=1).astyp...]
    dot_general x11 -> x0, matrix products: 15.8 us -> none  [the longest x1 3.75 us: body(): jnp.einsum('rd,fd->rf', flat_cot, weight_down, preferred_element_type=jnp...]
    all_gather x2 -> x0, blocking collectives: 14.8 us -> none  [the longest x1 7.42 us: body(): lax.all_gather(recv_cot, 'local', axis=2, tiled=True)]
    all_to_all x1 -> x0, blocking collectives: 14.2 us -> none  [body(): lax.all_to_all(outgoing, 'node', split_axis=2, concat_axis=2, tiled=True)]
    all_to_all x2 -> x0, starting transfers between devices: 10.6 us -> none  [the longest x1 7.25 us: body(): lax.all_to_all(send_tok, 'node', split_axis=0, concat_axis=0, tiled=True)]
    unnamed x14 -> x15, local copies, waits for them, and re-layouts: 0.04 us -> 8.98 us
    psum x1 -> x0, blocking collectives: 6.49 us -> none  [body(): weight_grad = lax.psum(partial_grad, 'local')]
  transfers between devices with their start and end apart: 3 -> 0, of which waited for: 2 -> 0; matrix products, arithmetic and copies ran while one was open for 5% -> 0% of each run, Pallas kernels for 0% -> 0%
where the time goes in v1:
time: 50 us; the launch traced here: 49.6 us
  Pallas kernels  40 us (80%)
  local copies, waits for them, and re-layouts  8.98 us (18%)
  between operations  0.66 us (1%)
    pallas_call x1, Pallas kernels, fused_body(): pl.pallas_call(functools.partial(fused_kernel, nodes), out_shape=(jax.Sha...  40 us
    unnamed x15, local copies, waits for them, and re-layouts  8.98 us

profile of v1, /device:TPU:0, one launch (start us, length us, event | category | flops | bytes accessed | tf_op | source)
XLA Modules:
  0.0 49.6 jit_solution(14646354171398456714)
XLA Ops:
  0.6 0.0 copy-start
  0.6 2.2 %copy-done = bf16[1,4096,512]{2,1,0:T(8,128)(2,1)S(1)} copy-done((bf16[1,4096,512]{2,1,0:T(8,128)(2,1)S(1)}, bf16[1,4096,512]{2,1,0:T(8,128)(2,1)}, u32[]{:S(2)}) %copy-start) | copy-done | bytes 4194328
  2.8 0.0 copy-start.1
  2.8 2.2 %copy-done.1 = bf16[1,4096,512]{2,1,0:T(8,128)(2,1)S(1)} copy-done((bf16[1,4096,512]{2,1,0:T(8,128)(2,1)S(1)}, bf16[1,4096,512]{2,1,0:T(8,128)(2,1)}, u32[]{:S(2)}) %copy-start.1) | copy-done | bytes 4194328
  5.0 0.0 copy-start.2
  5.0 0.7 %copy-done.2 = bf16[8,1024]{1,0:T(8,128)(2,1)S(1)} copy-done((bf16[8,1024]{1,0:T(8,128)(2,1)S(1)}, bf16[8,1024]{1,0:T(8,128)(2,1)}, u32[]{:S(2)}) %copy-start.2) | copy-done | bytes 16408
  5.7 0.0 copy-start.3
  5.7 0.7 %copy-done.3 = bf16[8,1024]{1,0:T(8,128)(2,1)S(1)} copy-done((bf16[8,1024]{1,0:T(8,128)(2,1)S(1)}, bf16[8,1024]{1,0:T(8,128)(2,1)}, u32[]{:S(2)}) %copy-start.3) | copy-done | bytes 16408
  6.4 0.0 copy-start.4
  6.4 0.7 %copy-done.4 = s32[8,8]{1,0:T(8,128)S(1)} copy-done((s32[8,8]{1,0:T(8,128)S(1)}, s32[8,8]{1,0:T(8,128)}, u32[]{:S(2)}) %copy-start.4) | copy-done | bytes 280
  7.1 0.0 copy-start.5
  7.1 0.7 %copy-done.5 = f32[8,8]{1,0:T(8,128)S(1)} copy-done((f32[8,8]{1,0:T(8,128)S(1)}, f32[8,8]{1,0:T(8,128)}, u32[]{:S(2)}) %copy-start.5) | copy-done | bytes 280
  7.8 40.0 %shard_map.94 = (bf16[8,1024]{1,0:T(8,128)(2,1)S(1)}, bf16[8,1024]{1,0:T(8,128)(2,1)S(1)}, f32[8,8]{1,0:T(8,128)S(1)}) custom-call(bf16[8,1024]{1,0:T(8,128)(2,1)S(1)} %copy-done.2, bf16[8,1024]{1,0:T(8,128)(2,1)S(1)} %copy-done.3, s32[8,8]{1,0:T(8,128)S(1)} %copy-done.4, f32[8,8]{1,0:T(8,128)S(1)} %copy-done.5, bf16[1,4096,512]{2,1,0:T(8,128)(2,1)S(1)} %copy-done, ...), custom_call_target="tpu_custom_call" | custom-call | tf_op jit(solution)/shard_map/pallas_call | solution.py:337
  47.8 0.6 %copy.13 = bf16[8,1024]{1,0:T(8,128)(2,1)} copy(bf16[8,1024]{1,0:T(8,128)(2,1)S(1)} %get-tuple-element.6) | data formatting | bytes 32768
  48.4 0.6 %copy.14 = bf16[8,1024]{1,0:T(8,128)(2,1)} copy(bf16[8,1024]{1,0:T(8,128)(2,1)S(1)} %get-tuple-element.7) | data formatting | bytes 32768
  49.0 0.6 %copy.15 = f32[8,8]{1,0:T(8,128)} copy(f32[8,8]{1,0:T(8,128)S(1)} %get-tuple-element.8) | data formatting | bytes 512
Async XLA Ops:
  0.6 2.2 %copy-start = (bf16[1,4096,512]{2,1,0:T(8,128)(2,1)S(1)}, bf16[1,4096,512]{2,1,0:T(8,128)(2,1)}, u32[]{:S(2)}) copy-start(bf16[1,4096,512]{2,1,0:T(8,128)(2,1)} %wg_hbm.1) | copy-start | bytes 12582916
  2.8 2.2 %copy-start.1 = (bf16[1,4096,512]{2,1,0:T(8,128)(2,1)S(1)}, bf16[1,4096,512]{2,1,0:T(8,128)(2,1)}, u32[]{:S(2)}) copy-start(bf16[1,4096,512]{2,1,0:T(8,128)(2,1)} %wu_hbm.1) | copy-start | bytes 12582916
  5.0 0.7 %copy-start.2 = (bf16[8,1024]{1,0:T(8,128)(2,1)S(1)}, bf16[8,1024]{1,0:T(8,128)(2,1)}, u32[]{:S(2)}) copy-start(bf16[8,1024]{1,0:T(8,128)(2,1)} %tok_ref.1) | copy-start | bytes 49156
  5.7 0.7 %copy-start.3 = (bf16[8,1024]{1,0:T(8,128)(2,1)S(1)}, bf16[8,1024]{1,0:T(8,128)(2,1)}, u32[]{:S(2)}) copy-start(bf16[8,1024]{1,0:T(8,128)(2,1)} %cot_ref.1) | copy-start | bytes 49156
  6.4 0.7 %copy-start.4 = (s32[8,8]{1,0:T(8,128)S(1)}, s32[8,8]{1,0:T(8,128)}, u32[]{:S(2)}) copy-start(s32[8,8]{1,0:T(8,128)} %ids_ref.1) | copy-start | bytes 772
  7.1 0.7 %copy-start.5 = (f32[8,8]{1,0:T(8,128)S(1)}, f32[8,8]{1,0:T(8,128)}, u32[]{:S(2)}) copy-start(f32[8,8]{1,0:T(8,128)} %cw_ref.1) | copy-start | bytes 772

commit v2 on v1

--- a/solution.py
+++ b/solution.py
@@ -93,16 +93,20 @@
 
 def fused_kernel(
     nodes,
-    tok_ref,
-    cot_ref,
-    ids_ref,
-    cw_ref,
+    tok_hbm,
+    cot_hbm,
+    ids_hbm,
+    cw_hbm,
     wg_hbm,
     wu_hbm,
     wd_hbm,
     lo_ref,
     tg_ref,
     wgrad_ref,
+    tok_ref,
+    cot_ref,
+    ids_ref,
+    cw_ref,
     wg_v,
     wu_v,
     wd_v,
@@ -118,6 +122,7 @@
     n_s,
     n_r,
     part,
+    in_sem,
     w_sem,
     xs_sem,
     xr_sem,
@@ -150,6 +155,18 @@
     def source(d):
         return lax.rem(me - d + nodes, nodes)
 
+    in_copies = []
+    in_pairs = ((tok_hbm, tok_ref), (cot_hbm, cot_ref), (ids_hbm, ids_ref), (cw_hbm, cw_ref))
+    for j, (far, near) in enumerate(in_pairs):
+        in_copies.append(pltpu.make_async_copy(far, near, in_sem.at[j]))
+        in_copies[j].start()
+
+    barrier = pltpu.get_barrier_semaphore()
+    for d in range(1, nodes):
+        pl.semaphore_signal(barrier, inc=1, device_id=(peer(d), l), device_id_type=MESH)
+    for c in (mate, ymate, diag):
+        pl.semaphore_signal(barrier, inc=1, device_id=(me, c), device_id_type=MESH)
+
     w_copies = []
     for j, c in enumerate(order):
         cols = pl.ds(pl.multiple_of(c * width, width), width)
@@ -162,12 +179,8 @@
             copy.start()
         w_copies.append(group)
 
-    barrier = pltpu.get_barrier_semaphore()
-    for d in range(1, nodes):
-        pl.semaphore_signal(barrier, inc=1, device_id=(peer(d), l), device_id_type=MESH)
-    for c in (mate, ymate, diag):
-        pl.semaphore_signal(barrier, inc=1, device_id=(me, c), device_id_type=MESH)
-
+    for copy in in_copies:
+        copy.wait()
     xb[l, me] = jnp.concatenate(
         [tok_ref[...].astype(jnp.float32), cot_ref[...].astype(jnp.float32)], axis=0
     ).astype(jnp.bfloat16)
@@ -219,14 +232,14 @@
     for d in range(1, nodes):
         x_node[d].wait_recv()
         onward(d)
-        relay(d - 1)
-    relay(nodes - 1)
 
     gate_pre = up_pre = grad_hidden = None
     for j, c in enumerate(order):
         for copy in w_copies[j]:
             copy.wait()
         if j == 1:
+            for d in range(nodes):
+                relay(d)
             for copy in x_mate:
                 copy.wait_recv()
         if j == 3:
@@ -325,6 +338,12 @@
         copy.wait_send()
 
 
+def write_kernel(a_ref, b_ref, c_ref, x_ref, y_ref, z_ref):
+    x_ref[...] = a_ref[...]
+    y_ref[...] = b_ref[...]
+    z_ref[...] = c_ref[...]
+
+
 def fused_body(tokens, cotangent, expert_ids, combine_weights, w_gate, w_up, w_down):
     nodes = lax.axis_size("node")
     toks, width = tokens.shape
@@ -333,17 +352,22 @@
     block = (nodes, 2 * toks, width)
     dma = pltpu.SemaphoreType.DMA
     vmem = pl.BlockSpec(memory_space=pltpu.VMEM)
-    hbm = pl.BlockSpec(memory_space=pl.ANY)
-    return pl.pallas_call(
+    hbm = pl.BlockSpec(memory_space=pltpu.HBM)
+    shapes = (
+        jax.ShapeDtypeStruct((toks, width), half),
+        jax.ShapeDtypeStruct((toks, width), half),
+        jax.ShapeDtypeStruct(expert_ids.shape, single),
+    )
+    results = pl.pallas_call(
         functools.partial(fused_kernel, nodes),
-        out_shape=(
-            jax.ShapeDtypeStruct((toks, width), half),
-            jax.ShapeDtypeStruct((toks, width), half),
-            jax.ShapeDtypeStruct(expert_ids.shape, single),
-        ),
-        in_specs=[vmem] * 4 + [hbm] * 3,
+        out_shape=shapes,
+        in_specs=[hbm] * 7,
         out_specs=(vmem, vmem, vmem),
         scratch_shapes=[
+            pltpu.VMEM((toks, width), half),
+            pltpu.VMEM((toks, width), half),
+            pltpu.VMEM(expert_ids.shape, jnp.int32),
+            pltpu.VMEM(combine_weights.shape, single),
             pltpu.VMEM((4, width, units), half),
             pltpu.VMEM((4, width, units), half),
             pltpu.VMEM((4, units, width), half),
@@ -359,6 +383,7 @@
             pltpu.VMEM(block, half),
             pltpu.VMEM(block, half),
             pltpu.VMEM(block, single),
+            dma((4,)),
             dma((3, 4)),
             dma((4, nodes)),
             dma((4, nodes)),
@@ -376,9 +401,12 @@
             dma((nodes,)),
         ],
         compiler_params=pltpu.CompilerParams(
-            collective_id=0, has_side_effects=True, vmem_limit_bytes=44 * 1024 * 1024
+            collective_id=0, has_side_effects=True, vmem_limit_bytes=62 * 1024 * 1024
         ),
     )(tokens, cotangent, expert_ids, combine_weights, w_gate, w_up, w_down)
+    return pl.pallas_call(
+        write_kernel, out_shape=shapes, in_specs=[vmem] * 3, out_specs=(vmem, vmem, vmem)
+    )(*results)
 
 
 def body(tokens, cotangent, expert_ids, combine_weights, w_gate, w_up, w_down):

time: 50 us -> 37.3 us (0.75)
  local copies, waits for them, and re-layouts: 8.98 us -> 0 us
  Pallas kernels: 40 us -> 36.3 us
    unnamed x15 -> x0, local copies, waits for them, and re-layouts: 8.98 us -> none
    pallas_call x1 -> x2, Pallas kernels: 40 us -> 36.3 us  [the longest x1 35 us: fused_body(): pl.pallas_call(functools.partial(fused_kernel, nodes), out_shape=shapes,...]
where the time goes in v2:
time: 37.3 us; the launch traced here: 37 us
  Pallas kernels  36.3 us (97%)
  between operations  0.64 us (2%)
    pallas_call x1, Pallas kernels, fused_body(): pl.pallas_call(functools.partial(fused_kernel, nodes), out_shape=shapes,...  35 us
    pallas_call x1, Pallas kernels, fused_body(): pl.pallas_call(write_kernel, out_shape=shapes, in_specs=[vmem] * 3, out_s...  1.35 us

profile of v2, /device:TPU:0, one launch (start us, length us, event | category | flops | bytes accessed | tf_op | source)
XLA Modules:
  0.0 37.0 jit_solution(8721051482541152058)
XLA Ops:
  0.6 35.0 %shard_map.94 = (bf16[8,1024]{1,0:T(8,128)(2,1)}, bf16[8,1024]{1,0:T(8,128)(2,1)}, f32[8,8]{1,0:T(8,128)}) custom-call(bf16[8,1024]{1,0:T(8,128)(2,1)} %tok_hbm.1, bf16[8,1024]{1,0:T(8,128)(2,1)} %cot_hbm.1, s32[8,8]{1,0:T(8,128)} %ids_hbm.1, f32[8,8]{1,0:T(8,128)} %cw_hbm.1, bf16[1,4096,512]{2,1,0:T(8,128)(2,1)} %wg_hbm.1, bf16[1,4096,512]{2,1,0:T(8,128)(2,1)} %wu_hbm.1, ...), custom_call_target="tpu_custom_call" | custom-call | tf_op jit(solution)/shard_map/pallas_call | solution.py:361
  35.6 1.4 %shard_map.95 = (bf16[8,1024]{1,0:T(8,128)(2,1)}, bf16[8,1024]{1,0:T(8,128)(2,1)}, f32[8,8]{1,0:T(8,128)}) custom-call(bf16[8,1024]{1,0:T(8,128)(2,1)} %get-tuple-element.6.a_ref, bf16[8,1024]{1,0:T(8,128)(2,1)} %get-tuple-element.7.b_ref, f32[8,8]{1,0:T(8,128)} %get-tuple-element.8.c_ref), custom_call_target="tpu_custom_call" | custom-call | tf_op jit(solution)/shard_map/pallas_call | solution.py:407

commit v3 on v2

--- a/solution.py
+++ b/solution.py
@@ -89,6 +89,16 @@
 
 def mm(a, b, dims):
     return lax.dot_general(a, b, dims, preferred_element_type=jnp.float32)
+
+
+def fold(x):
+    half = x.shape[-1] // 2
+    return jnp.concatenate([x[..., :half], x[..., half:]], axis=-2)
+
+
+def unfold(x):
+    half = x.shape[-2] // 2
+    return jnp.concatenate([x[..., :half, :], x[..., half:, :]], axis=-1)
 
 
 def fused_kernel(
@@ -181,9 +191,8 @@
 
     for copy in in_copies:
         copy.wait()
-    xb[l, me] = jnp.concatenate(
-        [tok_ref[...].astype(jnp.float32), cot_ref[...].astype(jnp.float32)], axis=0
-    ).astype(jnp.bfloat16)
+    for kind, ref in enumerate((tok_ref, cot_ref)):
+        xb[kind, l, me] = fold(ref[...].astype(jnp.float32)).astype(jnp.bfloat16)
     ids = ids_ref[...]
     lanes = lax.broadcasted_iota(jnp.int32, (toks, 128), 1)
     table = jnp.zeros((toks, 128), jnp.float32)
@@ -208,53 +217,67 @@
         sends.append(copy)
         return copy
 
-    x_node = [None]
+    x_node = {}
+    x_mate, x_y, x_diag = {}, {}, {}
+
+    def outward(kind):
+        for d in range(1, nodes):
+            block, q = xb.at[kind, l, me], 4 * kind
+            x_node[kind, d] = send(block, block, xs_sem.at[q, d], xr_sem.at[q, d], (peer(d), l))
+
+    def onward(kind, d):
+        if d:
+            x_node[kind, d].wait_recv()
+        block, q = xb.at[kind, l, source(d)], 4 * kind + 1
+        x_y[kind, d] = send(block, block, xs_sem.at[q, d], xr_sem.at[q, d], (me, ymate))
+
+    def inward(kind):
+        block, q = xb.at[kind, l], 4 * kind + 2
+        x_mate[kind] = send(block, block, xs_sem.at[q, 0], xr_sem.at[q, 0], (me, mate))
+
+    def relay(kind):
+        for d in range(nodes):
+            x_y[kind, d].wait_recv()
+        block, q = xb.at[kind, ymate], 4 * kind + 3
+        x_diag[kind] = send(block, block, xs_sem.at[q, 0], xr_sem.at[q, 0], (me, mate))
+
+    outward(0)
+    onward(0, 0)
+    outward(1)
     g_node = [None]
-    for d in range(1, nodes):
-        x_node.append(
-            send(xb.at[l, me], xb.at[l, me], xs_sem.at[0, d], xr_sem.at[0, d], (peer(d), l))
-        )
-    x_mate, x_y, x_diag = [], [], []
-
-    def onward(d):
-        block = xb.at[l, source(d)]
-        x_y.append(send(block, block, xs_sem.at[1, d], xr_sem.at[1, d], (me, ymate)))
-        x_mate.append(send(block, block, xs_sem.at[2, d], xr_sem.at[2, d], (me, mate)))
-
-    def relay(d):
-        x_y[d].wait_recv()
-        block = xb.at[ymate, source(d)]
-        x_diag.append(send(block, block, xs_sem.at[3, d], xr_sem.at[3, d], (me, mate)))
-
-    onward(0)
     for d in range(1, nodes):
         g_node.append(send(gt.at[me], gt.at[me], gs_sem.at[d], gr_sem.at[d], (peer(d), l)))
     for d in range(1, nodes):
-        x_node[d].wait_recv()
-        onward(d)
+        onward(0, d)
+    inward(0)
+    for d in range(nodes):
+        onward(1, d)
+    inward(1)
+
+    def features(kind, c):
+        whole = unfold(xb[kind, c].astype(jnp.float32))
+        return whole.reshape(rows, width).astype(jnp.bfloat16)
+
+    def arrived(kind, j):
+        if j == 1:
+            x_mate[kind].wait_recv()
+        if j == 3:
+            x_diag[kind].wait_recv()
 
     gate_pre = up_pre = grad_hidden = None
     for j, c in enumerate(order):
         for copy in w_copies[j]:
             copy.wait()
         if j == 1:
-            for d in range(nodes):
-                relay(d)
-            for copy in x_mate:
-                copy.wait_recv()
-        if j == 3:
-            for copy in x_diag:
-                copy.wait_recv()
-        both = xb[c].astype(jnp.float32).reshape(nodes, 2, toks, width)
-        tok = both[:, 0].reshape(rows, width).astype(jnp.bfloat16)
-        cot = both[:, 1].reshape(rows, width).astype(jnp.bfloat16)
+            relay(0)
+        arrived(0, j)
+        tok = features(0, c)
         a = mm(tok, wg_v[c], NN)
         b = mm(tok, wu_v[c], NN)
-        g = mm(cot, wd_v[c], NT)
         if j == 0:
-            gate_pre, up_pre, grad_hidden = a, b, g
+            gate_pre, up_pre = a, b
         else:
-            gate_pre, up_pre, grad_hidden = gate_pre + a, up_pre + b, grad_hidden + g
+            gate_pre, up_pre = gate_pre + a, up_pre + b
 
     for copy in g_node[1:]:
         copy.wait_recv()
@@ -263,38 +286,74 @@
     sigmoid = jax.nn.sigmoid(gate_pre)
     activated = gate_pre * sigmoid
     hidden = activated * up_pre
-    slope = sigmoid * (1.0 + gate_pre * (1.0 - sigmoid))
+    hid = (hidden * scale).astype(jnp.bfloat16)
+
+    def partial_out(c):
+        return fold(mm(hid, wd_v[c], NN).reshape(nodes, toks, width))
+
+    turns = list(range(1, nodes)) + [0]
+    y_copies, o_node, totals = {}, {}, {}
+
+    def to_mate(kind, i, value):
+        q = 2 * kind + i
+        mate_s[q] = value.astype(jnp.bfloat16)
+        return send(mate_s.at[q], mate_r.at[q], ms_sem.at[q], mr_sem.at[q], (me, mate))
+
+    def to_ymate(kind, value, first):
+        part[kind] = value
+        first.wait_recv()
+        y_s[kind] = (part[kind] + mate_r[2 * kind].astype(jnp.float32)).astype(jnp.bfloat16)
+        for d in turns:
+            n = peer(d)
+            y_copies[kind, d] = send(
+                y_s.at[kind, n], y_r.at[kind, n], ys_sem.at[kind, d], yr_sem.at[kind, d], (me, ymate)
+            )
+
+    def to_nodes(kind, second):
+        second.wait_recv()
+        for d in turns:
+            n = peer(d)
+            y_copies[kind, d].wait_recv()
+            value = part[kind, n] + mate_r[2 * kind + 1, n].astype(jnp.float32)
+            value = value + y_r[kind, n].astype(jnp.float32)
+            if d:
+                n_s[kind, d] = value.astype(jnp.bfloat16)
+                o_node[kind, d] = send(
+                    n_s.at[kind, d], n_r.at[kind, me], os_sem.at[kind, d], or_sem.at[kind, d], (n, l)
+                )
+            else:
+                totals[kind] = value
+
+    first = to_mate(0, 0, partial_out(diag))
+    to_ymate(0, partial_out(ymate), first)
+    second_out = to_mate(0, 1, partial_out(mate))
+    part[0] = partial_out(l)
+    relay(1)
+
+    for j, c in enumerate(order):
+        arrived(1, j)
+        g = mm(features(1, c), wd_v[c], NT)
+        grad_hidden = g if j == 0 else grad_hidden + g
     inner = jnp.sum(hidden * grad_hidden, axis=1, keepdims=True).reshape(nodes, toks, 1)
     nodes3 = lax.broadcasted_iota(jnp.int32, (nodes, toks, 128), 0)
     rl[l] = jnp.sum(jnp.where(lanes3 == nodes3, inner, 0.0), axis=0)
     r_local = []
     for j, c in enumerate((mate, ymate, diag)):
         r_local.append(send(rl.at[l], rl.at[l], ls_sem.at[j], lr_sem.at[j], (me, c)))
+    slope = sigmoid * (1.0 + gate_pre * (1.0 - sigmoid))
     scaled = grad_hidden * scale
-    hid = (hidden * scale).astype(jnp.bfloat16)
     ggate = (scaled * up_pre * slope).astype(jnp.bfloat16)
     gup = (scaled * activated).astype(jnp.bfloat16)
 
-    def partial(c):
-        out = mm(hid, wd_v[c], NN).reshape(nodes, toks, width)
-        into = (mm(ggate, wg_v[c], NT) + mm(gup, wu_v[c], NT)).reshape(nodes, toks, width)
-        return jnp.concatenate([out, into], axis=1)
-
-    def to_mate(i, c):
-        mate_s[i] = partial(c).astype(jnp.bfloat16)
-        return send(mate_s.at[i], mate_r.at[i], ms_sem.at[i], mr_sem.at[i], (me, mate))
-
-    first = to_mate(0, diag)
-    part[...] = partial(ymate)
-    first.wait_recv()
-    y_s[...] = (part[...] + mate_r[0].astype(jnp.float32)).astype(jnp.bfloat16)
-    turns = list(range(1, nodes)) + [0]
-    y_copies = {}
-    for d in turns:
-        n = peer(d)
-        y_copies[d] = send(y_s.at[n], y_r.at[n], ys_sem.at[d], yr_sem.at[d], (me, ymate))
-    second = to_mate(1, mate)
-    part[...] = partial(l)
+    def partial_in(c):
+        value = mm(ggate, wg_v[c], NT) + mm(gup, wu_v[c], NT)
+        return fold(value.reshape(nodes, toks, width))
+
+    first = to_mate(1, 0, partial_in(diag))
+    to_ymate(1, partial_in(ymate), first)
+    second_in = to_mate(1, 1, partial_in(mate))
+    to_nodes(0, second_out)
+    part[1] = partial_in(l)
 
     for copy in r_local:
         copy.wait_recv()
@@ -307,18 +366,7 @@
         if d:
             r_node.append(send(rn_s.at[d], rn.at[me], ns_sem.at[d], nr_sem.at[d], (n, l)))
 
-    second.wait_recv()
-    o_node = []
-    total = None
-    for d in turns:
-        n = peer(d)
-        y_copies[d].wait_recv()
-        value = part[n] + mate_r[1, n].astype(jnp.float32) + y_r[n].astype(jnp.float32)
-        if d:
-            n_s[d] = value.astype(jnp.bfloat16)
-            o_node.append(send(n_s.at[d], n_r.at[me], os_sem.at[d], or_sem.at[d], (n, l)))
-        else:
-            total = value
+    to_nodes(1, second_in)
     r_total = rn_s[0]
     for i, d in enumerate(range(1, nodes)):
         r_node[i].wait_recv()
@@ -329,11 +377,12 @@
         value = jnp.sum(jnp.where(lanes == ids[:, k : k + 1], r_total, 0.0), axis=1, keepdims=True)
         answer = answer + jnp.where(slots == k, value, 0.0)
     wgrad_ref[...] = answer
-    for i, d in enumerate(range(1, nodes)):
-        o_node[i].wait_recv()
-        total = total + n_r[source(d)].astype(jnp.float32)
-    lo_ref[...] = total[:toks].astype(jnp.bfloat16)
-    tg_ref[...] = total[toks:].astype(jnp.bfloat16)
+    for kind, ref in enumerate((lo_ref, tg_ref)):
+        total = totals[kind]
+        for d in range(1, nodes):
+            o_node[kind, d].wait_recv()
+            total = total + n_r[kind, source(d)].astype(jnp.float32)
+        ref[...] = unfold(total).astype(jnp.bfloat16)
     for copy in sends:
         copy.wait_send()
 
@@ -349,7 +398,7 @@
     toks, width = tokens.shape
     units = w_gate.shape[2]
     half, single = jnp.bfloat16, jnp.float32
-    block = (nodes, 2 * toks, width)
+    block = (nodes, 2 * toks, width // 2)
     dma = pltpu.SemaphoreType.DMA
     vmem = pl.BlockSpec(memory_space=pltpu.VMEM)
     hbm = pl.BlockSpec(memory_space=pltpu.HBM)
@@ -371,34 +420,34 @@
             pltpu.VMEM((4, width, units), half),
             pltpu.VMEM((4, width, units), half),
             pltpu.VMEM((4, units, width), half),
-            pltpu.VMEM((4,) + block, half),
+            pltpu.VMEM((2, 4) + block, half),
             pltpu.VMEM((nodes, toks, 128), single),
             pltpu.VMEM((4, toks, 128), single),
             pltpu.VMEM((nodes, toks, 128), single),
             pltpu.VMEM((nodes, toks, 128), single),
+            pltpu.VMEM((4,) + block, half),
+            pltpu.VMEM((4,) + block, half),
             pltpu.VMEM((2,) + block, half),
             pltpu.VMEM((2,) + block, half),
-            pltpu.VMEM(block, half),
-            pltpu.VMEM(block, half),
-            pltpu.VMEM(block, half),
-            pltpu.VMEM(block, half),
-            pltpu.VMEM(block, single),
+            pltpu.VMEM((2,) + block, half),
+            pltpu.VMEM((2,) + block, half),
+            pltpu.VMEM((2,) + block, single),
             dma((4,)),
             dma((3, 4)),
-            dma((4, nodes)),
-            dma((4, nodes)),
+            dma((8, nodes)),
+            dma((8, nodes)),
             dma((nodes,)),
             dma((nodes,)),
             dma((3,)),
             dma((3,)),
             dma((nodes,)),
             dma((nodes,)),
-            dma((2,)),
-            dma((2,)),
-            dma((nodes,)),
-            dma((nodes,)),
-            dma((nodes,)),
-            dma((nodes,)),
+            dma((4,)),
+            dma((4,)),
+            dma((2, nodes)),
+            dma((2, nodes)),
+            dma((2, nodes)),
+            dma((2, nodes)),
         ],
         compiler_params=pltpu.CompilerParams(
             collective_id=0, has_side_effects=True, vmem_limit_bytes=62 * 1024 * 1024

time: 37.3 us -> 36.3 us (0.973)
  Pallas kernels: 36.3 us -> 35.3 us
    pallas_call x1, Pallas kernels: 35 us -> 34 us  [fused_body(): pl.pallas_call(functools.partial(fused_kernel, nodes), out_shape=shapes,...]
where the time goes in v3:
time: 36.3 us; the launch traced here: 36 us
  Pallas kernels  35.3 us (97%)
  between operations  0.64 us (2%)
    pallas_call x1, Pallas kernels, fused_body(): pl.pallas_call(functools.partial(fused_kernel, nodes), out_shape=shapes,...  34 us
    pallas_call x1, Pallas kernels, fused_body(): pl.pallas_call(write_kernel, out_shape=shapes, in_specs=[vmem] * 3, out_s...  1.35 us

profile of v3, /device:TPU:0, one launch (start us, length us, event | category | flops | bytes accessed | tf_op | source)
XLA Modules:
  0.0 36.0 jit_solution(5519039483362531322)
XLA Ops:
  0.6 34.0 %shard_map.94 = (bf16[8,1024]{1,0:T(8,128)(2,1)}, bf16[8,1024]{1,0:T(8,128)(2,1)}, f32[8,8]{1,0:T(8,128)}) custom-call(bf16[8,1024]{1,0:T(8,128)(2,1)} %tok_hbm.1, bf16[8,1024]{1,0:T(8,128)(2,1)} %cot_hbm.1, s32[8,8]{1,0:T(8,128)} %ids_hbm.1, f32[8,8]{1,0:T(8,128)} %cw_hbm.1, bf16[1,4096,512]{2,1,0:T(8,128)(2,1)} %wg_hbm.1, bf16[1,4096,512]{2,1,0:T(8,128)(2,1)} %wu_hbm.1, ...), custom_call_target="tpu_custom_call" | custom-call | tf_op jit(solution)/shard_map/pallas_call | solution.py:410
  34.6 1.4 %shard_map.95 = (bf16[8,1024]{1,0:T(8,128)(2,1)}, bf16[8,1024]{1,0:T(8,128)(2,1)}, f32[8,8]{1,0:T(8,128)}) custom-call(bf16[8,1024]{1,0:T(8,128)(2,1)} %get-tuple-element.6.a_ref, bf16[8,1024]{1,0:T(8,128)(2,1)} %get-tuple-element.7.b_ref, f32[8,8]{1,0:T(8,128)} %get-tuple-element.8.c_ref), custom_call_target="tpu_custom_call" | custom-call | tf_op jit(solution)/shard_map/pallas_call | solution.py:456

commit v4 on v3

--- a/solution.py
+++ b/solution.py
@@ -351,8 +351,8 @@
 
     first = to_mate(1, 0, partial_in(diag))
     to_ymate(1, partial_in(ymate), first)
+    to_nodes(0, second_out)
     second_in = to_mate(1, 1, partial_in(mate))
-    to_nodes(0, second_out)
     part[1] = partial_in(l)
 
     for copy in r_local:

time: 36.3 us -> 35.5 us (0.978)
  Pallas kernels: 35.3 us -> 34.5 us
    pallas_call x1, Pallas kernels: 34 us -> 33.2 us  [fused_body(): pl.pallas_call(functools.partial(fused_kernel, nodes), out_shape=shapes,...]
where the time goes in v4:
time: 35.5 us; the launch traced here: 35.2 us
  Pallas kernels  34.5 us (97%)
  between operations  0.64 us (2%)
    pallas_call x1, Pallas kernels, fused_body(): pl.pallas_call(functools.partial(fused_kernel, nodes), out_shape=shapes,...  33.2 us
    pallas_call x1, Pallas kernels, fused_body(): pl.pallas_call(write_kernel, out_shape=shapes, in_specs=[vmem] * 3, out_s...  1.35 us

profile of v4, /device:TPU:0, one launch (start us, length us, event | category | flops | bytes accessed | tf_op | source)
XLA Modules:
  0.0 35.2 jit_solution(6612683120258729291)
XLA Ops:
  0.6 33.2 %shard_map.94 = (bf16[8,1024]{1,0:T(8,128)(2,1)}, bf16[8,1024]{1,0:T(8,128)(2,1)}, f32[8,8]{1,0:T(8,128)}) custom-call(bf16[8,1024]{1,0:T(8,128)(2,1)} %tok_hbm.1, bf16[8,1024]{1,0:T(8,128)(2,1)} %cot_hbm.1, s32[8,8]{1,0:T(8,128)} %ids_hbm.1, f32[8,8]{1,0:T(8,128)} %cw_hbm.1, bf16[1,4096,512]{2,1,0:T(8,128)(2,1)} %wg_hbm.1, bf16[1,4096,512]{2,1,0:T(8,128)(2,1)} %wu_hbm.1, ...), custom_call_target="tpu_custom_call" | custom-call | tf_op jit(solution)/shard_map/pallas_call | solution.py:410
  33.8 1.4 %shard_map.95 = (bf16[8,1024]{1,0:T(8,128)(2,1)}, bf16[8,1024]{1,0:T(8,128)(2,1)}, f32[8,8]{1,0:T(8,128)}) custom-call(bf16[8,1024]{1,0:T(8,128)(2,1)} %get-tuple-element.6.a_ref, bf16[8,1024]{1,0:T(8,128)(2,1)} %get-tuple-element.7.b_ref, f32[8,8]{1,0:T(8,128)} %get-tuple-element.8.c_ref), custom_call_target="tpu_custom_call" | custom-call | tf_op jit(solution)/shard_map/pallas_call | solution.py:456
